TPU v7x, 32 devices: a whole 2x2x4 slice. The times are simulated.
32 devices in a mesh: grp: 4 (over z), dp: 8 (over y, x, core).
Axes of the slice: x: 2, y: 2, z: 4, core: 2. Of those that a mesh axis runs over, the one named last changes fastest.
Arguments:
- audio: bfloat16 [32, 15360], P(('grp', 'dp')), may hold values from -6 to 6
- starts: int32 [96], P(('grp', 'dp')), may hold values from 0 to 12800
- offsets: int32 [32, 2, 32], P(('grp', 'dp')), may hold values from 0 to 383
- w_first: bfloat16 [10, 512], replicated, may hold values from -2 to 2
- w_second: bfloat16 [4096, 512], replicated, may hold values from -0.09375 to 0.09375
- gain: float32 [512], replicated, may hold values from 0.5 to 10, as said below
- w_context: bfloat16 [1024, 512], replicated, may hold values from -0.1875 to 0.1875
- w_predict: bfloat16 [2, 512, 512], replicated, may hold values from -0.25 to 0.25
Outputs:
- loss: float32 [], replicated
- grad_first: float32 [10, 512], replicated
- grad_second: float32 [4096, 512], P('dp')
- grad_gain: float32 [512], replicated
- grad_context: float32 [1024, 512], P('dp')
- grad_predict: float32 [2, 512, 512], P(None, 'dp')
Inputs may be any that keep to these rules, and one draw needn't show every extreme that they name: `starts`: first sample of a window. `offsets`: a latent row of the recording. `gain`: positive gains.
All inputs are finite; a program needn't handle non-finite values.
Results may differ from a plain program's by a relative error of at most 0.0085.
The roundings to bfloat16 on the way count: a program that leaves them out, or rounds other values in their place, can miss the bound.
Values may be sent and summed in bfloat16 or wider, within the bound.
A program may use at most 128 MiB of HBM per device.

v0:
```python
import math

import jax
import jax.numpy as jnp
from jax import lax
from jax.sharding import PartitionSpec as P

STEPS = 128


def shift_rows(values):
    return jnp.concatenate([jnp.zeros_like(values[:, :1]), values[:, :-1]], axis=1)


def shift_back(values):
    return jnp.concatenate([values[:, 1:], jnp.zeros_like(values[:, :1])], axis=1)


def future_rows(values, horizon):
    return jnp.concatenate([values[:, horizon:], jnp.zeros_like(values[:, :horizon])], axis=1)


def past_rows(values, horizon):
    return jnp.concatenate([jnp.zeros_like(values[:, :horizon]), values[:, :-horizon]], axis=1)


def encode(audio_row, starts_row, w_first, w_second, gain, w_context, w_predict):
    channels = w_second.shape[1]
    windows = starts_row.shape[0]
    span = 20 * STEPS
    waves = jax.vmap(lambda window_start: lax.dynamic_slice_in_dim(audio_row, window_start, span))(
        starts_row
    )
    frames = waves.reshape(windows, 4 * STEPS, 5)
    inputs_one = jnp.concatenate([shift_rows(frames), frames], axis=2).reshape(
        windows * 4 * STEPS, 10
    )
    pre_one = jnp.dot(inputs_one, w_first, preferred_element_type=jnp.float32)
    hidden_one = jax.nn.relu(pre_one).astype(jnp.bfloat16)
    grouped = hidden_one.reshape(windows, STEPS, 4 * channels)
    inputs_two = jnp.concatenate([shift_rows(grouped), grouped], axis=2).reshape(
        windows * STEPS, 8 * channels
    )
    pre_two = jnp.dot(inputs_two, w_second, preferred_element_type=jnp.float32)
    active = jax.nn.relu(pre_two)
    centred = active - jnp.mean(active, axis=1, keepdims=True)
    inv_std = lax.rsqrt(jnp.mean(centred * centred, axis=1, keepdims=True) + 1e-05)
    normed = centred * inv_std
    latent = (normed * gain).astype(jnp.bfloat16)
    latent_win = latent.reshape(windows, STEPS, channels)
    context_in = jnp.concatenate([shift_rows(latent_win), latent_win], axis=2).reshape(
        windows * STEPS, 2 * channels
    )
    context = jnp.dot(context_in, w_context, preferred_element_type=jnp.float32).astype(
        jnp.bfloat16
    )
    predicted = jnp.stack(
        [
            jnp.dot(context, w_predict[horizon_index], preferred_element_type=jnp.float32)
            for horizon_index in range(w_predict.shape[0])
        ]
    ).astype(jnp.bfloat16)
    return (
        inputs_one,
        pre_one,
        inputs_two,
        pre_two,
        normed,
        inv_std,
        latent,
        context_in,
        context,
        predicted,
    )


def head(latent, predicted, panel, valid_total, scale):
    channels = latent.shape[1]
    windows = latent.shape[0] // STEPS
    latent_win = latent.reshape(windows, STEPS, channels)
    loss_sum = jnp.zeros((), jnp.float32)
    grad_latent = jnp.zeros((windows, STEPS, channels), jnp.float32)
    weight_list = []
    query_list = []
    for horizon_index in range(predicted.shape[0]):
        horizon = horizon_index + 1
        query = predicted[horizon_index]
        target = future_rows(latent_win, horizon).reshape(windows * STEPS, channels)
        valid = jnp.tile((jnp.arange(STEPS) + horizon < STEPS).astype(jnp.float32), windows)
        positive = jnp.sum(query.astype(jnp.float32) * target.astype(jnp.float32), axis=1) * scale
        panel_rows = panel[:, horizon_index, :]
        negative = jnp.dot(query, panel_rows.T, preferred_element_type=jnp.float32) * scale
        highest = jnp.maximum(positive, jnp.max(negative, axis=1))
        denominator = jnp.exp(positive - highest) + jnp.sum(
            jnp.exp(negative - highest[:, None]), axis=1
        )
        log_total = highest + jnp.log(denominator)
        loss_sum = loss_sum + jnp.sum(valid * (log_total - positive))
        pos_grad = valid * (jnp.exp(positive - log_total) - 1.0) * (scale / valid_total)
        neg_weights = (
            valid[:, None] * jnp.exp(negative - log_total[:, None]) * (scale / valid_total)
        ).astype(jnp.bfloat16)
        query_grad = (
            pos_grad[:, None] * target.astype(jnp.float32)
            + jnp.dot(neg_weights, panel_rows, preferred_element_type=jnp.float32)
        ).astype(jnp.bfloat16)
        grad_latent = grad_latent + past_rows(
            (pos_grad[:, None] * query.astype(jnp.float32)).reshape(windows, STEPS, channels),
            horizon,
        )
        weight_list.append(neg_weights)
        query_list.append(query_grad)
    return (
        loss_sum,
        jnp.stack(weight_list),
        jnp.stack(query_list),
        grad_latent.reshape(windows * STEPS, channels),
    )


def add_own(grad_latent, picks, owned):
    for horizon_index in range(picks.shape[0]):
        grad_latent = grad_latent.at[picks[horizon_index]].add(owned[:, horizon_index, :])
    return grad_latent


def backward(saved, grad_latent, query_grads, w_second, gain, w_context, w_predict):
    (
        inputs_one,
        pre_one,
        inputs_two,
        pre_two,
        normed,
        inv_std,
        latent,
        context_in,
        context,
        predicted,
    ) = saved
    channels = w_second.shape[1]
    windows = latent.shape[0] // STEPS
    grad_predict = jnp.stack(
        [
            jnp.dot(context.T, query_grads[horizon_index], preferred_element_type=jnp.float32)
            for horizon_index in range(w_predict.shape[0])
        ]
    )
    context_sum = jnp.dot(query_grads[0], w_predict[0].T, preferred_element_type=jnp.float32)
    horizon_index = 1
    context_sum = context_sum + jnp.dot(
        query_grads[horizon_index], w_predict[horizon_index].T, preferred_element_type=jnp.float32
    )
    context_grad = context_sum.astype(jnp.bfloat16)
    grad_context = jnp.dot(context_in.T, context_grad, preferred_element_type=jnp.float32)
    back_in = jnp.dot(context_grad, w_context.T, preferred_element_type=jnp.float32).reshape(
        windows, STEPS, 2 * channels
    )
    latent_total = (
        grad_latent.reshape(windows, STEPS, channels)
        + back_in[:, :, channels:]
        + shift_back(back_in[:, :, :channels])
    )
    latent_total = latent_total.reshape(windows * STEPS, channels)
    grad_gain = jnp.sum(latent_total * normed, axis=0)
    normed_grad = latent_total * gain
    active_grad = inv_std * (
        normed_grad
        - jnp.mean(normed_grad, axis=1, keepdims=True)
        - normed * jnp.mean(normed_grad * normed, axis=1, keepdims=True)
    )
    pre_two_grad = jnp.where(pre_two > 0, active_grad, 0.0).astype(jnp.bfloat16)
    grad_second = jnp.dot(inputs_two.T, pre_two_grad, preferred_element_type=jnp.float32)
    back_two = jnp.dot(pre_two_grad, w_second.T, preferred_element_type=jnp.float32).reshape(
        windows, STEPS, 8 * channels
    )
    grouped_grad = back_two[:, :, 4 * channels :] + shift_back(back_two[:, :, : 4 * channels])
    hidden_grad = grouped_grad.reshape(windows * 4 * STEPS, channels)
    pre_one_grad = jnp.where(pre_one > 0, hidden_grad, 0.0).astype(jnp.bfloat16)
    grad_first = jnp.dot(inputs_one.T, pre_one_grad, preferred_element_type=jnp.float32)
    return (grad_first, grad_second, grad_gain, grad_context, grad_predict)


def on_device(audio, starts, offsets, w_first, w_second, gain, w_context, w_predict):
    channels = w_second.shape[1]
    horizons = w_predict.shape[0]
    scale = 1.0 / math.sqrt(channels)
    groups = lax.axis_size("grp")
    shards = lax.axis_size("dp")
    windows = starts.shape[0]
    valid_total = float(
        windows * groups * shards * (horizons * STEPS - horizons * (horizons + 1) // 2)
    )
    saved = encode(audio[0], starts, w_first, w_second, gain, w_context, w_predict)
    latent = saved[6]
    predicted = saved[9]
    picks = offsets[0]
    chosen = latent[picks].transpose(1, 0, 2)
    panel = lax.all_gather(chosen, "dp", axis=0, tiled=True)
    loss_sum, neg_weights, query_grads, grad_latent = head(
        latent, predicted, panel, valid_total, scale
    )
    owned = lax.psum_scatter(
        jnp.einsum("ktn,ktd->nkd", neg_weights, predicted, preferred_element_type=jnp.float32),
        "dp",
        scatter_dimension=0,
        tiled=True,
    )
    grad_latent = add_own(grad_latent, picks, owned)
    grad_first, grad_second, grad_gain, grad_context, grad_predict = backward(
        saved, grad_latent, query_grads, w_second, gain, w_context, w_predict
    )
    grad_first, grad_gain, loss_sum = lax.psum((grad_first, grad_gain, loss_sum), ("grp", "dp"))
    grad_second, grad_context, grad_predict = (
        lax.psum_scatter(grad_second, "dp", scatter_dimension=0, tiled=True),
        lax.psum_scatter(grad_context, "dp", scatter_dimension=0, tiled=True),
        lax.psum_scatter(grad_predict, "dp", scatter_dimension=1, tiled=True),
    )
    grad_second, grad_context, grad_predict = (
        lax.psum(grad_second.astype(jnp.bfloat16), "grp").astype(jnp.float32),
        lax.psum(grad_context.astype(jnp.bfloat16), "grp").astype(jnp.float32),
        lax.psum(grad_predict.astype(jnp.bfloat16), "grp").astype(jnp.float32),
    )
    return (loss_sum / valid_total, grad_first, grad_second, grad_gain, grad_context, grad_predict)


def solution(mesh):
    return jax.shard_map(
        on_device,
        mesh=mesh,
        in_specs=(
            P(("grp", "dp"), None),
            P(("grp", "dp")),
            P(("grp", "dp"), None, None),
            P(),
            P(),
            P(),
            P(),
            P(),
        ),
        out_specs=(P(), P(), P("dp", None), P(), P("dp", None), P(None, "dp", None)),
        check_vma=False,
    )
```

profile of v0, /device:TPU:0, one launch (start us, length us, event | category | flops | bytes accessed | tf_op | source)
XLA Modules:
  0.0 341.1 jit_solution(3017475548930438679)
XLA Ops:
  8.9 1.0 reduce.9
  9.9 4.4 %while.1 = (s32[]{:T(128)}, bf16[15360]{0:T(1024)(128)(2,1)S(1)}, s32[3,1]{0,1:T(1,128)S(1)}, bf16[3,2560]{1,0:T(4,128)(2,1)S(1)}, s32[]{:T(128)}, /*index=5*/s32[]{:T(128)}) while((s32[]{:T(128)}, bf16[15360]{0:T(1024)(128)(2,1)S(1)}, s32[3,1]{0,1:T(1,128)S(1)}, bf16[3,2560]{1,0:T(4,128)(2,1)S(1)}, s32[]{:T(128)}, /*index=5*/s32[]{:T(128)}) %tuple.37), condition=%wide.while_cond, body=%wide.while_body.sunk | while | flops 2 | bytes 30817 | solution.py:31
  10.5 0.7 dynamic-slice.13
  12.0 0.7 dynamic-slice.13
  13.4 0.7 dynamic-slice.13
  15.0 0.7 reshape.303
  16.2 3.0 maximum_convert_fusion
  19.2 2.3 concatenate.55
  21.5 2.2 reshape.304
  23.7 1.9 concatenate.53
  25.6 4.7 %maximum_reduce_fusion = (f32[384]{0:T(512)S(1)}, f32[384,512]{1,0:T(8,128)S(1)}) fusion(bf16[4096,512]{1,0:T(8,128)(2,1)} %param.12, bf16[384,2048]{1,0:T(8,128)(2,1)S(1)} %copy-done.3, bf16[384,2048]{1,0:T(8,128)(2,1)S(1)} %bitcast.196), kind=kOutput, calls=%fused_computation.51 | convolution fusion | flops 1617297024 | bytes 8128000 | tf_op jit(solution)/shard_map/dot_general | solution.py:44
  31.0 0.8 fusion.72
  31.9 1.3 gather_fusion
  33.3 11.7 %all_gather.3 = bf16[256,2,512]{2,0,1:T(8,128)(2,1)S(1)} all-gather(bf16[32,2,512]{2,0,1:T(8,128)(2,1)} %bitcast.210), channel_id=1, replica_groups=mesh['grp'=4,'dp'=8] {'dp'}, dimensions={0}, use_global_device_ids=true | all-gather | bytes 589824 | tf_op jit(solution)/shard_map/all_gather | solution.py:198
  51.0 1.5 convolution_bitcast_fusion.2
  52.5 2.3 copy.24
  54.8 1.4 fusion.6
  56.2 1.5 fusion.5
  58.9 1.5 pad_maximum_fusion.1
  60.6 1.5 fusion.16
  62.1 1.4 fusion.4
  63.5 0.7 copy-done.7
  64.3 2.1 fusion.19
  68.1 1.6 fusion.75
  69.7 1.0 slice.106
  70.9 1.1 pad_add_fusion
  72.0 39.8 %all-reduce.15.cloned.1.call-done = f32[256,2,512]{2,1,0:T(2,128)} async-done(((f32[256,2,512]{2,1,0:T(2,128)}), f32[256,2,512]{2,1,0:T(2,128)}) %all-reduce.15.cloned.1.call-update) | async-done | bytes 1048592
  111.9 1.1 constant_dynamic-slice_fusion.2
  113.0 2.8 scatter_custom_fusion
  115.7 2.8 scatter_custom_fusion.1
  118.5 1.9 multiply_reduce_fusion.1
  121.1 5.6 %fusion = f32[4096,512]{1,0:T(8,128)} fusion(bf16[384,512]{1,0:T(8,128)(2,1)S(1)} %select_convert_fusion.2, bf16[384,2048]{1,0:T(8,128)(2,1)S(1)} %copy-done.4, bf16[384,2048]{1,0:T(8,128)(2,1)S(1)} %bitcast.197), kind=kOutput, calls=%fused_computation.9 | convolution fusion | flops 1616904192 | bytes 11927552 | tf_op jit(solution)/shard_map/dot_general | solution.py:172
  129.3 4.0 %fusion.76 = f32[384,4096]{1,0:T(8,128)S(1)} fusion(bf16[384,512]{1,0:T(8,128)(2,1)S(1)} %select_convert_fusion.2, bf16[4096,512]{1,0:T(8,128)(2,1)} %param.12), kind=kOutput, calls=%fused_computation.147 | convolution fusion | flops 1610612736 | bytes 10878976 | tf_op jit(solution)/shard_map/dot_general | solution.py:173
  133.4 2.7 copy-done.2
  136.1 2.0 slice.108
  138.0 17.4 %reduce-scatter.8.cloned.1.call-done = f32[2,64,512]{2,1,0:T(8,128)} async-done(((f32[2,512,512]{2,1,0:T(8,128)}), f32[2,64,512]{2,1,0:T(8,128)}) %reduce-scatter.8.cloned.1.call-update) | async-done | bytes 262160 | tf_op jit(solution)/shard_map/reduce_scatter | solution.py:216
  155.4 1.6 convert_element_type.135
  157.1 43.3 %reduce-scatter.6.cloned.1.call-done = f32[128,512]{1,0:T(8,128)} async-done(((f32[1024,512]{1,0:T(8,128)}), f32[128,512]{1,0:T(8,128)}) %reduce-scatter.6.cloned.1.call-update) | async-done | bytes 262160 | tf_op jit(solution)/shard_map/reduce_scatter | solution.py:215
  200.3 1.6 convert_element_type.133
  202.0 73.0 %reduce-scatter.4.cloned.1.call-done = f32[512,512]{1,0:T(8,128)} async-done(((f32[4096,512]{1,0:T(8,128)}), f32[512,512]{1,0:T(8,128)}) %reduce-scatter.4.cloned.1.call-update) | async-done | bytes 1048592 | tf_op jit(solution)/shard_map/reduce_scatter | solution.py:214
  275.0 2.1 convert_element_type.131
  277.1 4.5 %slice_add_fusion = bf16[3,128,2048]{2,1,0:T(8,128)(2,1)} fusion(f32[3,128,4096]{2,1,0:T(8,128)} %bitcast.190, f32[3,127,2048]{2,1,0:T(8,128)} %slice.108), kind=kLoop, calls=%fused_computation.4 | loop fusion | flops 1572864 | bytes 7839744 | tf_op jit(solution)/shard_map/add | solution.py:176
  281.6 2.8 reshape.311
  284.4 2.4 fusion.2
  286.8 40.6 %all-reduce.10 = (f32[]{:T(128)}, f32[10,512]{1,0:T(8,128)}, f32[512]{0:T(512)}) all-reduce(f32[]{:T(128)S(6)} %add.238, f32[10,512]{1,0:T(8,128)S(1)} %fusion.2, f32[512]{0:T(512)S(1)} %get-tuple-element.14), channel_id=1, replica_groups=mesh['grp'=4,'dp'=8] {'grp','dp'}, use_global_device_ids=true, to_apply=%region_10.11 | all-reduce | flops 5633 | bytes 45064 | tf_op jit(solution)/shard_map/psum | solution.py:212
  328.0 1.6 convert_element_type.134
  329.7 1.6 convert_element_type.136
  331.3 2.1 convert_element_type.132
  (156 shorter events, 16.2 us)
Async XLA Ops:
  7.2 38.0 %copy-start = (bf16[1024,512]{1,0:T(8,128)(2,1)S(1)}, bf16[1024,512]{1,0:T(8,128)(2,1)}, u32[]{:S(2)}) copy-start(bf16[1024,512]{1,0:T(8,128)(2,1)} %param.14) | copy-start | bytes 3145732
  7.2 104.7 %all-reduce.15.cloned.1.call-start = ((), (), s32[]{:S(2)}) async-start(), calls=%async_computation.6 | async-start | bytes 2097152
  15.8 5.6 %copy-start.24 = (bf16[1536,5]{0,1:T(8,128)(2,1)}, bf16[1536,5]{0,1:T(8,128)(2,1)S(1)}, u32[]{:S(2)}) copy-start(bf16[1536,5]{0,1:T(8,128)(2,1)S(1)} %copy.21) | copy-start | bytes 46084
  16.2 5.3 %copy-start.26 = (bf16[1536,5]{0,1:T(8,128)(2,1)}, bf16[1536,5]{0,1:T(8,128)(2,1)S(1)}, u32[]{:S(2)}) copy-start(bf16[1536,5]{0,1:T(8,128)(2,1)S(1)} %copy.20) | copy-start | bytes 46084
  23.7 1.9 copy-start.3
  25.6 4.7 %copy-start.5 = (bf16[3,128,2048]{2,1,0:T(8,128)(2,1)}, bf16[3,128,2048]{2,1,0:T(8,128)(2,1)S(1)}, u32[]{:S(2)}) copy-start(bf16[3,128,2048]{2,1,0:T(8,128)(2,1)S(1)} %concatenate.53) | copy-start | bytes 4718596
  25.6 5.0 %copy-start.28 = (f32[512]{0:T(512)S(1)}, f32[512]{0:T(512)}, u32[]{:S(2)}) copy-start(f32[512]{0:T(512)} %param.13) | copy-start | bytes 6148
  30.3 1.5 copy-start.43
  33.3 12.5 %copy-start.21 = (bf16[2,512,512]{2,1,0:T(8,128)(2,1)S(1)}, bf16[2,512,512]{2,1,0:T(8,128)(2,1)}, u32[]{:S(2)}) copy-start(bf16[2,512,512]{2,1,0:T(8,128)(2,1)} %param.15) | copy-start | bytes 3145732
  33.3 12.9 %copy-start.22 = (bf16[3,128,512]{2,1,0:T(8,128)(2,1)}, bf16[3,128,512]{2,1,0:T(8,128)(2,1)S(1)}, u32[]{:S(2)}) copy-start(bf16[3,128,512]{2,1,0:T(8,128)(2,1)S(1)} %concatenate.61) | copy-start | bytes 1179652
  45.1 1.1 copy-start.12
  45.1 1.6 copy-start.41
  45.2 2.8 copy-start.18
  45.8 2.7 copy-start.8
  46.2 4.7 %copy-start.14 = (bf16[384,512]{1,0:T(8,128)(2,1)}, bf16[384,512]{1,0:T(8,128)(2,1)S(1)}, u32[]{:S(2)}) copy-start(bf16[384,512]{1,0:T(8,128)(2,1)S(1)} %get-tuple-element.55) | copy-start | bytes 1179652
  46.3 2.9 copy-start.39
  47.3 3.6 %copy-start.37 = (f32[384]{0:T(512)}, f32[384]{0:T(512)S(1)}, u32[]{:S(2)}) copy-start(f32[384]{0:T(512)S(1)} %get-tuple-element.45) | copy-start | bytes 4612
  47.9 2.5 copy-start.31
  48.0 0.7 copy-start.23
  48.5 1.9 copy-start.29
  48.5 2.5 copy-start.16
  49.8 1.2 copy-start.38
  54.8 100.7 %reduce-scatter.8.cloned.1.call-start = ((), (), s32[]{:S(2)}) async-start(), calls=%async_computation.5 | async-start | bytes 2359296 | tf_op jit(solution)/shard_map/reduce_scatter | solution.py:216
  54.8 2.9 copy-start.9
  56.2 1.5 copy-start.10
  57.7 0.7 copy-start.19
  58.9 1.6 copy-start.20
  58.9 3.1 copy-start.11
  60.5 3.8 %copy-start.13 = (bf16[3,128,512]{2,1,0:T(8,128)(2,1)S(1)}, bf16[3,128,512]{2,1,0:T(8,128)(2,1)}, u32[]{:S(2)}) copy-start(bf16[3,128,512]{2,1,0:T(8,128)(2,1)} %copy-done.12) | copy-start | bytes 1179652
  60.5 139.8 %reduce-scatter.6.cloned.1.call-start = ((), (), s32[]{:S(2)}) async-start(), calls=%async_computation.4 | async-start | bytes 2359296 | tf_op jit(solution)/shard_map/reduce_scatter | solution.py:215
  63.5 0.7 copy-start.7
  64.3 2.4 copy-start.45
  64.3 3.6 %copy-start.17 = (bf16[384,512]{1,0:T(8,128)(2,1)S(1)}, bf16[384,512]{1,0:T(8,128)(2,1)}, u32[]{:S(2)}) copy-start(bf16[384,512]{1,0:T(8,128)(2,1)} %copy-done.16) | copy-start | bytes 1179652
  64.3 3.7 %copy-start.15 = (bf16[384,512]{1,0:T(8,128)(2,1)S(1)}, bf16[384,512]{1,0:T(8,128)(2,1)}, u32[]{:S(2)}) copy-start(bf16[384,512]{1,0:T(8,128)(2,1)} %copy-done.14) | copy-start | bytes 1179652
  66.4 208.6 %reduce-scatter.4.cloned.1.call-start = ((), (), s32[]{:S(2)}) async-start(), calls=%async_computation.3 | async-start | bytes 9437184 | tf_op jit(solution)/shard_map/reduce_scatter | solution.py:214
  68.0 2.7 copy-start.36
  68.1 2.7 copy-start.35
  70.7 1.3 copy-start.44
  118.5 2.6 copy-start.4
  118.5 2.6 copy-start.6
  126.7 0.7 copy-start.32
  126.7 0.7 copy-start.34
  126.7 0.7 copy-start.40
  126.8 201.2 %all-reduce.17.cloned.1.call-start = ((), (), s32[]{:S(2)}) async-start(), calls=%async_computation.7 | async-start | bytes 1572864 | tf_op jit(solution)/shard_map/psum | solution.py:219
  133.4 2.7 copy-start.2
  281.6 2.8 copy-start.25
  281.6 2.8 copy-start.27
  284.4 49.1 %copy-start.1 = (bf16[1024,512]{1,0:T(8,128)(2,1)S(1)}, bf16[1024,512]{1,0:T(8,128)(2,1)}, u32[]{:S(2)}) copy-start(bf16[1024,512]{1,0:T(8,128)(2,1)} %param.14) | copy-start | bytes 3145732
  (3 other events, 1.9 us)
Sparse Core Ops, SparseCore 0:
  54.9 56.9 all-reduce.14
  115.1 40.2 reduce-scatter.7
  159.1 41.2 reduce-scatter.5
  203.6 71.2 reduce-scatter.3
  278.1 45.0 all-reduce.16
where the time goes:
time: 342 us; the launch traced here: 341 us
  waiting for transfers between devices  174 us (51%)
  blocking collectives  52.3 us (15%)
  matrix products  33.7 us (10%)
  other arithmetic  32.9 us (10%)
  local copies, waits for them, and re-layouts  29.9 us (9%)
  between operations  18.1 us (5%)
    reduce_scatter x1, waiting for transfers between devices, on_device(): lax.psum_scatter(grad_second, 'dp', scatter_dimension=0, tiled=True)  73 us
    reduce_scatter x1, waiting for transfers between devices, on_device(): lax.psum_scatter(grad_context, 'dp', scatter_dimension=0, tiled=True)  43.3 us
    psum x1, blocking collectives, on_device(): lax.psum((grad_first, grad_gain, loss_sum), ('grp', 'dp'))  40.6 us
    unnamed x6, waiting for transfers between devices  39.9 us
    reduce_scatter x1, waiting for transfers between devices, on_device(): lax.psum_scatter(grad_predict, 'dp', scatter_dimension=1, tiled=True)  17.4 us
    all_gather x1, blocking collectives, on_device(): panel = lax.all_gather(chosen, 'dp', axis=0, tiled=True)  11.7 us
  transfers between devices with their start and end apart: 5, of which 4 were waited for; matrix products, arithmetic and copies ran while one was open for 14% of the time, Pallas kernels for 0%

commit v1 on v0

v1 whole, which is shorter than its diff:
```python
import functools
import math

import jax
import jax.numpy as jnp
from jax import lax
from jax.experimental import pallas as pl
from jax.experimental.pallas import tpu as pltpu
from jax.sharding import PartitionSpec as P

STEPS = 128
LANES = 128
F32 = jnp.float32
BF16 = jnp.bfloat16
MESH = pl.DeviceIdType.MESH


def dot(a, b):
    return lax.dot_general(a, b, (((1,), (0,)), ((), ())), preferred_element_type=F32)


def dot_nt(a, b):
    return lax.dot_general(a, b, (((1,), (1,)), ((), ())), preferred_element_type=F32)


def dot_tn(a, b):
    return lax.dot_general(a, b, (((0,), (0,)), ((), ())), preferred_element_type=F32)


def later(values, by):
    row = lax.broadcasted_iota(jnp.int32, values.shape, 0)
    return jnp.where(row >= by, pltpu.roll(values, by, 0), 0.0)


def earlier(values, by):
    row = lax.broadcasted_iota(jnp.int32, values.shape, 0)
    return jnp.where(row < STEPS - by, pltpu.roll(values, STEPS - by, 0), 0.0)


def kernel(
    n, g, count,
    offs_ref, xq_ref, w1_ref, w2_ref, gain_ref, wc_ref, wp_ref,
    gs_ref, gc_ref, gp_ref, small_ref,
    hid, acc_a, acc_b, pre2, normed, inv, latent, context, pred, negs, negw, posq, qg, glat, cgv, pv, gfirst,
    panel, own_out, own_in, loss_acc, small_in, small_z,
    stage, core_in, chip_in, z_out, z_in, fin,
    panel_s, panel_r, own_s, own_r, sdp_s, sdp_r, sz_s, sz_r,
    core_s, core_r, chip_s, chip_r, z_s, z_r, f_s, f_r,
):
    tokens, channels = latent.shape
    wins = tokens // STEPS
    horizons = wp_ref.shape[0]
    pieces, _, chips, prow, _ = stage.shape
    picks = offs_ref.shape[0]
    per = picks // horizons
    cols = channels // g
    scale = 1.0 / math.sqrt(channels)
    me = lax.axis_index("dp")
    zme = lax.axis_index("grp")
    my_core = lax.rem(me, 2)
    my_chip = me // 2
    quarters = hid.shape[0]

    def dp_peer(j):
        return lax.rem(me + j, n)

    def z_peer(j):
        return lax.rem(zme + j, g)

    def chip_peer(j):
        return lax.rem(my_chip + j, chips)

    def each(size, body):
        def step(j, carry):
            body(j)
            return carry

        lax.fori_loop(1, size, step, 0)

    def windows(body):
        def step(w, carry):
            body(pl.ds(pl.multiple_of(w * STEPS, STEPS), STEPS))
            return carry

        lax.fori_loop(0, wins, step, 0)

    barrier = pltpu.get_barrier_semaphore()
    each(n, lambda j: pl.semaphore_signal(barrier, inc=1, device_id={"dp": dp_peer(j)}, device_id_type=MESH))
    each(g, lambda j: pl.semaphore_signal(barrier, inc=1, device_id={"grp": z_peer(j)}, device_id_type=MESH))

    def to_dp(src, dst, ssem, rsem, peer):
        return pltpu.make_async_remote_copy(
            src_ref=src, dst_ref=dst, send_sem=ssem, recv_sem=rsem, device_id={"dp": peer}, device_id_type=MESH
        )

    def to_z(src, dst, ssem, rsem, peer):
        return pltpu.make_async_remote_copy(
            src_ref=src, dst_ref=dst, send_sem=ssem, recv_sem=rsem, device_id={"grp": peer}, device_id_type=MESH
        )

    acc_a[...] = jnp.zeros_like(acc_a)
    acc_b[...] = jnp.zeros_like(acc_b)

    def quarter(q, carry):
        h = jnp.maximum(dot(xq_ref[q], w1_ref[...]), 0.0).astype(BF16)
        hid[q] = h
        acc_a[...] += dot(h, w2_ref[q])
        acc_b[...] += dot(h, w2_ref[q + quarters])
        return carry

    lax.fori_loop(0, quarters, quarter, 0)

    def norm(rows):
        pre = later(acc_a[rows, :], 1) + acc_b[rows, :]
        pre2[rows, :] = pre
        active = jnp.maximum(pre, 0.0)
        centred = active - jnp.mean(active, axis=1, keepdims=True)
        inv_std = lax.rsqrt(jnp.mean(centred * centred, axis=1, keepdims=True) + 1e-05)
        norm_row = centred * inv_std
        normed[rows, :] = norm_row
        inv[rows, :] = inv_std
        latent[rows, :] = (norm_row * gain_ref[...]).astype(BF16)

    windows(norm)

    place = lax.broadcasted_iota(jnp.int32, (picks, tokens), 1)
    chosen = jnp.where(place == offs_ref[...], 1.0, 0.0).astype(BF16)
    panel[me] = dot(chosen, latent[...]).astype(BF16)
    pl.semaphore_wait(barrier, n - 1 + g - 1)

    def panel_copy(j, slot):
        return to_dp(panel.at[slot], panel.at[slot], panel_s.at[j], panel_r.at[slot], dp_peer(j))

    each(n, lambda j: panel_copy(j, me).start())

    acc_a[...] = dot(latent[...], wc_ref[0])
    acc_b[...] = dot(latent[...], wc_ref[1])

    def make_context(rows):
        context[rows, :] = (later(acc_a[rows, :], 1) + acc_b[rows, :]).astype(BF16)

    windows(make_context)
    for k in range(horizons):
        pred[k] = dot(context[...], wp_ref[k]).astype(BF16)
    glat[...] = jnp.zeros_like(glat)
    loss_acc[...] = jnp.zeros_like(loss_acc)
    each(n, lambda j: panel_copy(j, dp_peer(j)).wait_recv())

    def panel_rows(k):
        return panel[:, k * per : (k + 1) * per, :].reshape(n * per, channels)

    for k in range(horizons):
        negs[...] = dot_nt(pred[k], panel_rows(k)) * scale

        def head(rows, k=k):
            query = pred[k, rows, :].astype(F32)
            target = earlier(latent[rows, :].astype(F32), k + 1)
            step = lax.broadcasted_iota(jnp.int32, (STEPS, 1), 0)
            valid = jnp.where(step + (k + 1) < STEPS, 1.0, 0.0)
            positive = jnp.sum(query * target, axis=1, keepdims=True) * scale
            negative = negs[rows, :]
            highest = jnp.maximum(positive, jnp.max(negative, axis=1, keepdims=True))
            denominator = jnp.exp(positive - highest) + jnp.sum(
                jnp.exp(negative - highest), axis=1, keepdims=True
            )
            log_total = highest + jnp.log(denominator)
            lost = jnp.sum(valid * (log_total - positive), axis=0, keepdims=True)
            loss_acc[...] += jnp.broadcast_to(lost, loss_acc.shape)
            pos_grad = valid * (jnp.exp(positive - log_total) - 1.0) * (scale / count)
            negw[k, rows, :] = (valid * jnp.exp(negative - log_total) * (scale / count)).astype(BF16)
            posq[k, rows, :] = pos_grad * target
            glat[rows, :] += later(pos_grad * query, k + 1)

        windows(head)
        owed = dot_tn(negw[k], pred[k]).astype(BF16)
        own_out[:, k * per : (k + 1) * per, :] = owed.reshape(n, per, channels)

    def own_copy(j, slot):
        return to_dp(own_out.at[dp_peer(j)], own_in.at[slot], own_s.at[j], own_r.at[slot], dp_peer(j))

    each(n, lambda j: own_copy(j, me).start())

    def core_copy(p):
        return to_dp(stage.at[p, 1 - my_core], core_in.at[p], core_s.at[p], core_r.at[p], me + 1 - 2 * my_core)

    def chip_copy(p, j, slot):
        c = chip_peer(j)
        return to_dp(
            stage.at[p, my_core, c], chip_in.at[p, slot], chip_s.at[p, j], chip_r.at[p, slot], c * 2 + my_core
        )

    def z_copy(p, j, slot):
        return to_z(z_out.at[p, z_peer(j)], z_in.at[p, slot], z_s.at[p, j], z_r.at[p, slot], z_peer(j))

    def fin_copy(p, j, slot):
        return to_z(fin.at[p, slot], fin.at[p, slot], f_s.at[p, j], f_r.at[p, slot], z_peer(j))

    def core_done(p):
        core_copy(p).wait_recv()

        def add(c, carry):
            total = stage[p, my_core, c].astype(F32) + core_in[p, c].astype(F32)
            stage[p, my_core, c] = total.astype(BF16)
            return carry

        lax.fori_loop(0, chips, add, 0)
        each(chips, lambda j: chip_copy(p, j, my_chip).start())

    def chip_done(p):
        each(chips, lambda j: chip_copy(p, j, chip_peer(j)).wait_recv())

        def add(j, total):
            return total + chip_in[p, chip_peer(j)].astype(F32)

        total = lax.fori_loop(1, chips, add, stage[p, my_core, my_chip].astype(F32)).astype(BF16)
        for z in range(g):
            z_out[p, z] = total[:, z * cols : (z + 1) * cols]
        each(g, lambda j: z_copy(p, j, zme).start())

    def z_done(p):
        each(g, lambda j: z_copy(p, j, z_peer(j)).wait_recv())

        def add(j, total):
            return total + z_in[p, z_peer(j)].astype(F32)

        fin[p, zme] = lax.fori_loop(1, g, add, z_out[p, zme].astype(F32)).astype(BF16)
        each(g, lambda j: fin_copy(p, j, zme).start())

    def fin_done(p):
        each(g, lambda j: fin_copy(p, j, z_peer(j)).wait_recv())
        for z in range(g):
            at = slice(z * cols, (z + 1) * cols)
            value = fin[p, z].astype(F32)
            if p == 0:
                part = prow // horizons
                for k in range(horizons):
                    gp_ref[k, :, at] = value[k * part : (k + 1) * part]
            elif p == 1:
                gc_ref[:, at] = value
            else:
                gs_ref[(p - 2) * prow : (p - 1) * prow, at] = value

    shares = []
    for k in range(horizons):
        qg[k] = (posq[k] + dot(negw[k], panel_rows(k))).astype(BF16)
        shares.append(dot_tn(context[...], qg[k]).reshape(n, channels // n, channels))
    joined = jnp.concatenate(shares, axis=1).astype(BF16).reshape(chips, 2, prow, channels)
    for parity in range(2):
        stage[0, parity] = joined[:, parity]
    core_copy(0).start()

    acc_a[...] = dot_nt(qg[0], wp_ref[0])
    for k in range(1, horizons):
        acc_a[...] += dot_nt(qg[k], wp_ref[k])

    def make_context_grad(rows):
        rounded = acc_a[rows, :].astype(BF16)
        cgv[1, rows, :] = rounded
        cgv[0, rows, :] = earlier(rounded.astype(F32), 1).astype(BF16)

    windows(make_context_grad)
    for half in range(2):
        share = dot_tn(latent[...], cgv[half]).astype(BF16).reshape(chips // 2, 2, prow, channels)
        for parity in range(2):
            stage[1, parity, half * (chips // 2) : (half + 1) * (chips // 2)] = share[:, parity]
    core_copy(1).start()
    acc_a[...] = dot_nt(cgv[1], wc_ref[1]) + dot_nt(cgv[0], wc_ref[0])

    each(n, lambda j: own_copy(j, dp_peer(j)).wait_recv())
    owned = lax.fori_loop(
        1, n, lambda j, total: total + own_in[dp_peer(j)].astype(F32), own_out[me].astype(F32)
    )
    high = owned.astype(BF16)
    low = (owned - high.astype(F32)).astype(BF16)
    acc_b[...] = dot_tn(chosen, high) + dot_tn(chosen, low)
    core_done(0)
    core_done(1)
    small_in[me] = jnp.zeros_like(small_in[me])
    gfirst[...] = jnp.zeros_like(gfirst)

    def norm_back(rows):
        total = glat[rows, :] + acc_a[rows, :] + acc_b[rows, :]
        norm_row = normed[rows, :]
        small_in[me, 0:1] += jnp.sum(total * norm_row, axis=0, keepdims=True)
        grad = total * gain_ref[...]
        active_grad = inv[rows, :] * (
            grad
            - jnp.mean(grad, axis=1, keepdims=True)
            - norm_row * jnp.mean(grad * norm_row, axis=1, keepdims=True)
        )
        rounded = jnp.where(pre2[rows, :] > 0, active_grad, 0.0).astype(BF16)
        pv[1, rows, :] = rounded
        pv[0, rows, :] = earlier(rounded.astype(F32), 1).astype(BF16)

    windows(norm_back)

    blocks = channels // LANES
    seconds = pieces - 2

    def second(b, i):
        lhs = hid[lax.rem(b, quarters), :, i * LANES : (i + 1) * LANES]
        return dot_tn(lhs, pv[b // quarters]).astype(BF16)

    if prow == LANES:
        for i in range(seconds):

            def fill(b, carry, i=i):
                stage[2 + i, lax.rem(b, 2), b // 2] = second(b, i)
                return carry

            lax.fori_loop(0, 2 * quarters, fill, 0)
            core_copy(2 + i).start()
            if i > 0:
                core_done(1 + i)
    else:
        each_chips = LANES // (seconds * prow) // 2

        def fill(b, carry):
            for i in range(blocks):
                share = second(b, i).reshape(each_chips, 2, seconds, prow, channels)
                at = pl.ds((b * blocks + i) * each_chips, each_chips)
                for parity in range(2):
                    for s in range(seconds):
                        stage[2 + s, parity, at] = share[:, parity, s]
            return carry

        lax.fori_loop(0, 2 * quarters, fill, 0)
        for i in range(seconds):
            core_copy(2 + i).start()
            if i > 0:
                core_done(1 + i)
    core_done(pieces - 1)
    chip_done(0)
    chip_done(1)

    def first(q, carry):
        back = dot_nt(pv[1], w2_ref[q + quarters]) + dot_nt(pv[0], w2_ref[q])
        pre = dot(xq_ref[q], w1_ref[...])
        gfirst[...] += dot_tn(xq_ref[q], jnp.where(pre > 0, back, 0.0).astype(BF16))
        return carry

    lax.fori_loop(0, quarters, first, 0)
    row = lax.broadcasted_iota(jnp.int32, (16, channels), 0)
    gain_row = small_in[me, 0:1]
    small_in[me] = (
        jnp.where(row < 10, gfirst[0:16, :], 0.0)
        + jnp.where(row == 10, gain_row, 0.0)
        + jnp.where(row == 11, loss_acc[...], 0.0)
    )

    def small_copy(j, slot):
        return to_dp(small_in.at[slot], small_in.at[slot], sdp_s.at[j], sdp_r.at[slot], dp_peer(j))

    def small_z_copy(j, slot):
        return to_z(small_z.at[slot], small_z.at[slot], sz_s.at[j], sz_r.at[slot], z_peer(j))

    each(n, lambda j: small_copy(j, me).start())
    chip_done(2)
    z_done(0)
    z_done(1)
    each(n, lambda j: small_copy(j, dp_peer(j)).wait_recv())
    small_z[zme] = lax.fori_loop(1, n, lambda j, total: total + small_in[j], small_in[0])
    each(g, lambda j: small_z_copy(j, zme).start())
    for p in range(3, pieces):
        chip_done(p)
        z_done(p - 1)
        fin_done(p - 3)
    z_done(pieces - 1)
    each(g, lambda j: small_z_copy(j, z_peer(j)).wait_recv())
    small_ref[...] = lax.fori_loop(1, g, lambda j, total: total + small_z[j], small_z[0])
    for p in range(pieces - 3, pieces):
        fin_done(p)

    def leave_dp(j):
        panel_copy(j, me).wait_send()
        own_copy(j, me).wait_send()
        small_copy(j, me).wait_send()

    each(n, leave_dp)
    each(g, lambda j: small_z_copy(j, zme).wait_send())
    for p in range(pieces):
        core_copy(p).wait_send()
        each(chips, lambda j, p=p: chip_copy(p, j, my_chip).wait_send())

        def leave_z(j, p=p):
            z_copy(p, j, zme).wait_send()
            fin_copy(p, j, zme).wait_send()

        each(g, leave_z)


def frame_inputs(audio_row, starts, channels):
    span = 20 * STEPS
    rows = []
    for w in range(starts.shape[0]):
        wave = lax.dynamic_slice_in_dim(audio_row, starts[w], span)
        steps = wave.reshape(STEPS, 20)
        before = jnp.concatenate([jnp.zeros((1, 5), wave.dtype), steps[:-1, 15:]], axis=0)
        rows.append(jnp.concatenate([before, steps], axis=1))
    wide = jnp.concatenate(rows, axis=0)
    parts = [jnp.pad(wide[:, 5 * q : 5 * q + 10], ((0, 0), (0, LANES - 10))) for q in range(4)]
    return jnp.stack(parts)


def on_device(audio, starts, offsets, w_first, w_second, gain, w_context, w_predict):
    channels = w_second.shape[1]
    horizons = w_predict.shape[0]
    g = lax.axis_size("grp")
    n = lax.axis_size("dp")
    wins = starts.shape[0]
    tokens = wins * STEPS
    count = float(wins * g * n * (horizons * STEPS - horizons * (horizons + 1) // 2))
    xq = frame_inputs(audio[0], starts, channels)
    w1 = jnp.pad(w_first, ((0, LANES - w_first.shape[0]), (0, 0)))
    picks = offsets.shape[1] * offsets.shape[2]
    offs = offsets.reshape(picks, 1)
    quarters = w_second.shape[0] // (2 * channels)
    prow = 2 * channels // n
    pieces = 2 + w_second.shape[0] // (2 * channels)
    chips = n // 2
    cols = channels // g
    panel_width = n * offsets.shape[2]
    vm = pltpu.VMEM
    dma = pltpu.SemaphoreType.DMA
    spec = pl.BlockSpec(memory_space=pltpu.VMEM)
    full = (tokens, channels)
    gs, gc, gp, small = pl.pallas_call(
        functools.partial(kernel, n, g, count),
        out_shape=(
            jax.ShapeDtypeStruct((w_second.shape[0] // n, channels), F32),
            jax.ShapeDtypeStruct((w_context.shape[0] // n, channels), F32),
            jax.ShapeDtypeStruct((horizons, channels // n, channels), F32),
            jax.ShapeDtypeStruct((16, channels), F32),
        ),
        in_specs=[spec] * 7,
        out_specs=[spec] * 4,
        scratch_shapes=[
            vm((quarters,) + full, BF16),
            vm(full, F32),
            vm(full, F32),
            vm(full, F32),
            vm(full, F32),
            vm((tokens, 1), F32),
            vm(full, BF16),
            vm(full, BF16),
            vm((horizons,) + full, BF16),
            vm((tokens, panel_width), F32),
            vm((horizons, tokens, panel_width), BF16),
            vm((horizons,) + full, F32),
            vm((horizons,) + full, BF16),
            vm(full, F32),
            vm((2,) + full, BF16),
            vm((2,) + full, BF16),
            vm((LANES, channels), F32),
            vm((n, picks, channels), BF16),
            vm((n, picks, channels), BF16),
            vm((n, picks, channels), BF16),
            vm((1, channels), F32),
            vm((n, 16, channels), F32),
            vm((g, 16, channels), F32),
            vm((pieces, 2, chips, prow, channels), BF16),
            vm((pieces, chips, prow, channels), BF16),
            vm((pieces, chips, prow, channels), BF16),
            vm((pieces, g, prow, cols), BF16),
            vm((pieces, g, prow, cols), BF16),
            vm((pieces, g, prow, cols), BF16),
        ]
        + [dma((n,))] * 6
        + [dma((g,))] * 2
        + [dma((pieces,))] * 2
        + [dma((pieces, chips))] * 2
        + [dma((pieces, g))] * 4,
        compiler_params=pltpu.CompilerParams(
            collective_id=0, has_side_effects=True, vmem_limit_bytes=56 * 1024 * 1024
        ),
    )(
        offs,
        xq,
        w1,
        w_second.reshape(2 * quarters, channels, channels),
        gain.reshape(1, channels),
        w_context.reshape(2, channels, channels),
        w_predict,
    )
    return (small[11, 0] / count, small[:10], gs, small[10], gc, gp)


def solution(mesh):
    return jax.shard_map(
        on_device,
        mesh=mesh,
        in_specs=(
            P(("grp", "dp"), None),
            P(("grp", "dp")),
            P(("grp", "dp"), None, None),
            P(),
            P(),
            P(),
            P(),
            P(),
        ),
        out_specs=(P(), P(), P("dp", None), P(), P("dp", None), P(None, "dp", None)),
        check_vma=False,
    )
```

time: 342 us -> 121 us (0.35)
  waiting for transfers between devices: 174 us -> 0 us
  Pallas kernels: 0 us -> 94.8 us
  blocking collectives: 52.3 us -> 0 us
  matrix products: 33.7 us -> 0 us
  other arithmetic: 32.9 us -> 0.91 us
  local copies, waits for them, and re-layouts: 29.9 us -> 16.4 us
  between operations: 18.1 us -> 8.32 us
    reduce_scatter x3 -> x0, waiting for transfers between devices: 134 us -> none  [the longest x1 73 us: on_device(): lax.psum_scatter(grad_second, 'dp', scatter_dimension=0, tiled=True)]
    pallas_call x0 -> x1, Pallas kernels: none -> 94.8 us  [on_device(): pl.pallas_call(functools.partial(kernel, n, g, count), out_shape=(jax.Sha...]
    psum x1 -> x0, blocking collectives: 40.6 us -> none  [on_device(): lax.psum((grad_first, grad_gain, loss_sum), ('grp', 'dp'))]
    unnamed x6 -> x0, waiting for transfers between devices: 39.9 us -> none
    dot_general x19 -> x0, matrix products: 33.7 us -> none  [the longest x1 5.62 us: backward(): jnp.dot(inputs_two.T, pre_two_grad, preferred_element_type=jnp.float32)]
    convert_element_type x12 -> x0, other arithmetic: 12.5 us -> none  [the longest x1 2.14 us: on_device(): lax.psum(grad_second.astype(jnp.bfloat16), 'grp').astype(jnp.float32)]
    all_gather x1 -> x0, blocking collectives: 11.7 us -> none  [on_device(): panel = lax.all_gather(chosen, 'dp', axis=0, tiled=True)]
    gather x13 -> x0, local copies, waits for them, and re-layouts: 5.61 us -> none
  transfers between devices with their start and end apart: 5 -> 0, of which waited for: 4 -> 0; matrix products, arithmetic and copies ran while one was open for 14% -> 0% of each run, Pallas kernels for 0% -> 0%
where the time goes in v1:
time: 121 us; the launch traced here: 120 us
  Pallas kernels  94.8 us (78%)
  local copies, waits for them, and re-layouts  16.4 us (14%)
  between operations  8.32 us (7%)
    pallas_call x1, Pallas kernels, on_device(): pl.pallas_call(functools.partial(kernel, n, g, count), out_shape=(jax.Sha...  94.8 us
    unnamed x11, local copies, waits for them, and re-layouts  7.82 us
    slice x2, local copies, waits for them, and re-layouts, on_device(): return (small[11, 0] / count, small[:10], gs, small[10], gc, gp)  2.5 us

profile of v1, /device:TPU:0, one launch (start us, length us, event | category | flops | bytes accessed | tf_op | source)
XLA Modules:
  0.0 120.3 jit_solution(10068534966658010413)
XLA Ops:
  0.6 1.4 %fusion.16 = (s32[1]{0:T(128)}, s32[1]{0:T(128)}, s32[1]{0:T(128)}) fusion(s32[3]{0:T(128)} %param.9), kind=kLoop, calls=%fused_computation.29 | loop fusion | bytes 24 | tf_op jit(solution)/shard_map/slice | solution.py:396
  7.8 0.9 dynamic-slice_reduce_fusion.2
  8.7 0.1 reshape.42
  8.8 0.1 slice.52
  8.9 0.1 copy.31
  9.0 0.1 reshape.43
  9.1 0.1 slice.53
  9.2 0.1 copy.32
  9.3 0.1 reshape.44
  9.4 0.1 slice.54
  9.5 0.1 copy.33
  9.6 0.1 copy.17
  9.7 0.1 copy.19
  9.8 0.1 copy.21
  9.9 0.1 fusion.12
  10.0 0.1 copy.27
  10.2 0.1 copy.28
  10.4 0.1 copy.29
  10.5 0.1 copy.30
  10.7 0.8 pad_maximum_fusion.xq_ref
  11.5 1.4 %pad.24.w1_ref = bf16[128,512]{1,0:T(8,128)(2,1)} pad(bf16[10,512]{1,0:T(8,128)(2,1)} %param.11, bf16[]{:T(256)} %constant.12.clone.1), padding=0_118x0_0 | pad | bytes 141314 | tf_op jit(solution)/shard_map/jit(_pad)/pad | solution.py:414
  12.9 1.4 %reshape.48.offs_ref = s32[64,1]{1,0:T(8,128)} reshape(s32[1,2,32]{2,1,0:T(2,128)} %param.10) | data formatting | bytes 512 | tf_op jit(solution)/shard_map/reshape | solution.py:416
  14.3 94.8 %shard_map.127 = (f32[512,512]{1,0:T(8,128)}, f32[128,512]{1,0:T(8,128)}, f32[2,64,512]{2,1,0:T(8,128)}, f32[16,512]{1,0:T(8,128)}) custom-call(s32[64,1]{1,0:T(8,128)} %reshape.48.offs_ref, bf16[4,384,128]{2,1,0:T(8,128)(2,1)} %pad_maximum_fusion.xq_ref, bf16[128,512]{1,0:T(8,128)(2,1)} %pad.24.w1_ref, bf16[8,512,512]{2,1,0:T(8,128)(2,1)} %bitcast.17, ...), custom_call_target="tpu_custom_call" | custom-call | tf_op jit(solution)/shard_map/pallas_call | solution.py:427
  109.1 1.3 %slice.51 = f32[1,512]{1,0:T(1,128)} slice(f32[16,512]{1,0:T(8,128)} %get-tuple-element.10), slice={[10:11], [0:512]} | slice | bytes 4096 | tf_op jit(solution)/shard_map/slice | solution.py:485
  110.4 1.2 slice.49
  112.2 1.4 %copy.38 = f32[10,512]{1,0:T(8,128)} copy(f32[10,512]{1,0:T(8,128)} %bitcast.19) | data formatting | bytes 40960
  113.6 2.3 %copy.39 = f32[512,512]{1,0:T(8,128)} copy(f32[512,512]{1,0:T(8,128)} %get-tuple-element.36) | data formatting | bytes 2097152
  115.9 1.7 %copy.40 = f32[128,512]{1,0:T(8,128)} copy(f32[128,512]{1,0:T(8,128)} %get-tuple-element.38) | data formatting | bytes 524288
  117.5 1.7 %copy.41 = f32[2,64,512]{2,1,0:T(8,128)} copy(f32[2,64,512]{2,1,0:T(8,128)} %get-tuple-element.39) | data formatting | bytes 524288
  (3 shorter events, 0.1 us)

commit v2 on v1

--- a/solution.py
+++ b/solution.py
@@ -39,11 +39,11 @@
 
 def kernel(
     n, g, count,
-    offs_ref, xq_ref, w1_ref, w2_ref, gain_ref, wc_ref, wp_ref,
-    gs_ref, gc_ref, gp_ref, small_ref,
-    hid, acc_a, acc_b, pre2, normed, inv, latent, context, pred, negs, negw, posq, qg, glat, cgv, pv, gfirst,
+    offs_ref, x_ref, first_ref, w2_ref, gain_ref, wc_ref, wp_ref,
+    fin, small_ref,
+    w1, hid, acc_a, acc_b, pre2, normed, inv, latent, context, pred, negs, negw, posq, qg, glat, cgv, pv, gfirst, w1f,
     panel, own_out, own_in, loss_acc, small_in, small_z,
-    stage, core_in, chip_in, z_out, z_in, fin,
+    stage, core_in, chip_in, z_out, z_in,
     panel_s, panel_r, own_s, own_r, sdp_s, sdp_r, sz_s, sz_r,
     core_s, core_r, chip_s, chip_r, z_s, z_r, f_s, f_r,
 ):
@@ -51,8 +51,7 @@
     wins = tokens // STEPS
     horizons = wp_ref.shape[0]
     pieces, _, chips, prow, _ = stage.shape
-    picks = offs_ref.shape[0]
-    per = picks // horizons
+    per = offs_ref.shape[2]
     cols = channels // g
     scale = 1.0 / math.sqrt(channels)
     me = lax.axis_index("dp")
@@ -98,11 +97,17 @@
             src_ref=src, dst_ref=dst, send_sem=ssem, recv_sem=rsem, device_id={"grp": peer}, device_id_type=MESH
         )
 
+    taps = first_ref.shape[0]
+    w1f[...] = jnp.zeros_like(w1f)
+    for q in range(quarters):
+        w1f[q, taps // 2 * q : taps // 2 * q + taps, :] = first_ref[...].astype(F32)
+    w1[...] = w1f[...].astype(BF16)
+
     acc_a[...] = jnp.zeros_like(acc_a)
     acc_b[...] = jnp.zeros_like(acc_b)
 
     def quarter(q, carry):
-        h = jnp.maximum(dot(xq_ref[q], w1_ref[...]), 0.0).astype(BF16)
+        h = jnp.maximum(dot(x_ref[...], w1[q]), 0.0).astype(BF16)
         hid[q] = h
         acc_a[...] += dot(h, w2_ref[q])
         acc_b[...] += dot(h, w2_ref[q + quarters])
@@ -123,9 +128,10 @@
 
     windows(norm)
 
-    place = lax.broadcasted_iota(jnp.int32, (picks, tokens), 1)
-    chosen = jnp.where(place == offs_ref[...], 1.0, 0.0).astype(BF16)
-    panel[me] = dot(chosen, latent[...]).astype(BF16)
+    place = lax.broadcasted_iota(jnp.int32, (tokens, per), 0)
+    chosen = [jnp.where(place == offs_ref[0, k : k + 1, :], 1.0, 0.0).astype(BF16) for k in range(horizons)]
+    for k in range(horizons):
+        panel[me, k * per : (k + 1) * per] = dot_tn(chosen[k], latent[...]).astype(BF16)
     pl.semaphore_wait(barrier, n - 1 + g - 1)
 
     def panel_copy(j, slot):
@@ -228,17 +234,6 @@
 
     def fin_done(p):
         each(g, lambda j: fin_copy(p, j, z_peer(j)).wait_recv())
-        for z in range(g):
-            at = slice(z * cols, (z + 1) * cols)
-            value = fin[p, z].astype(F32)
-            if p == 0:
-                part = prow // horizons
-                for k in range(horizons):
-                    gp_ref[k, :, at] = value[k * part : (k + 1) * part]
-            elif p == 1:
-                gc_ref[:, at] = value
-            else:
-                gs_ref[(p - 2) * prow : (p - 1) * prow, at] = value
 
     shares = []
     for k in range(horizons):
@@ -272,11 +267,13 @@
     )
     high = owned.astype(BF16)
     low = (owned - high.astype(F32)).astype(BF16)
-    acc_b[...] = dot_tn(chosen, high) + dot_tn(chosen, low)
+    acc_b[...] = jnp.zeros_like(acc_b)
+    for k in range(horizons):
+        mine = slice(k * per, (k + 1) * per)
+        acc_b[...] += dot(chosen[k], high[mine]) + dot(chosen[k], low[mine])
     core_done(0)
     core_done(1)
     small_in[me] = jnp.zeros_like(small_in[me])
-    gfirst[...] = jnp.zeros_like(gfirst)
 
     def norm_back(rows):
         total = glat[rows, :] + acc_a[rows, :] + acc_b[rows, :]
@@ -335,15 +332,18 @@
 
     def first(q, carry):
         back = dot_nt(pv[1], w2_ref[q + quarters]) + dot_nt(pv[0], w2_ref[q])
-        pre = dot(xq_ref[q], w1_ref[...])
-        gfirst[...] += dot_tn(xq_ref[q], jnp.where(pre > 0, back, 0.0).astype(BF16))
+        pre = dot(x_ref[...], w1[q])
+        gfirst[q] = dot_tn(x_ref[...], jnp.where(pre > 0, back, 0.0).astype(BF16))
         return carry
 
     lax.fori_loop(0, quarters, first, 0)
     row = lax.broadcasted_iota(jnp.int32, (16, channels), 0)
     gain_row = small_in[me, 0:1]
+    first_sum = gfirst[0, 0:16, :]
+    for q in range(1, quarters):
+        first_sum = first_sum + gfirst[q, taps // 2 * q : taps // 2 * q + 16, :]
     small_in[me] = (
-        jnp.where(row < 10, gfirst[0:16, :], 0.0)
+        jnp.where(row < 10, first_sum, 0.0)
         + jnp.where(row == 10, gain_row, 0.0)
         + jnp.where(row == 11, loss_acc[...], 0.0)
     )
@@ -389,17 +389,33 @@
         each(g, leave_z)
 
 
-def frame_inputs(audio_row, starts, channels):
+def finish(count, fin_ref, small_ref, loss_ref, gf_ref, gs_ref, gg_ref, gc_ref, gp_ref):
+    pieces, g, prow, cols = fin_ref.shape
+    horizons, part, _ = gp_ref.shape
+    for z in range(g):
+        at = slice(z * cols, (z + 1) * cols)
+        value = fin_ref[0, z].astype(F32)
+        for k in range(horizons):
+            gp_ref[k, :, at] = value[k * part : (k + 1) * part]
+        gc_ref[:, at] = fin_ref[1, z].astype(F32)
+        for p in range(2, pieces):
+            gs_ref[(p - 2) * prow : (p - 1) * prow, at] = fin_ref[p, z].astype(F32)
+    gf_ref[...] = small_ref[0:10, :]
+    gg_ref[...] = small_ref[10:11, :]
+    loss_ref[...] = small_ref[11:12, 0:1] / count
+
+
+def frame_inputs(audio, starts):
     span = 20 * STEPS
     rows = []
     for w in range(starts.shape[0]):
-        wave = lax.dynamic_slice_in_dim(audio_row, starts[w], span)
+        wave = lax.dynamic_slice(
+            audio, (jnp.int32(0), starts[w]), (1, span), allow_negative_indices=False
+        )
         steps = wave.reshape(STEPS, 20)
         before = jnp.concatenate([jnp.zeros((1, 5), wave.dtype), steps[:-1, 15:]], axis=0)
         rows.append(jnp.concatenate([before, steps], axis=1))
-    wide = jnp.concatenate(rows, axis=0)
-    parts = [jnp.pad(wide[:, 5 * q : 5 * q + 10], ((0, 0), (0, LANES - 10))) for q in range(4)]
-    return jnp.stack(parts)
+    return jnp.pad(jnp.concatenate(rows, axis=0), ((0, 0), (0, LANES - 25)))
 
 
 def on_device(audio, starts, offsets, w_first, w_second, gain, w_context, w_predict):
@@ -410,10 +426,8 @@
     wins = starts.shape[0]
     tokens = wins * STEPS
     count = float(wins * g * n * (horizons * STEPS - horizons * (horizons + 1) // 2))
-    xq = frame_inputs(audio[0], starts, channels)
-    w1 = jnp.pad(w_first, ((0, LANES - w_first.shape[0]), (0, 0)))
+    x = frame_inputs(audio, starts)
     picks = offsets.shape[1] * offsets.shape[2]
-    offs = offsets.reshape(picks, 1)
     quarters = w_second.shape[0] // (2 * channels)
     prow = 2 * channels // n
     pieces = 2 + w_second.shape[0] // (2 * channels)
@@ -424,17 +438,16 @@
     dma = pltpu.SemaphoreType.DMA
     spec = pl.BlockSpec(memory_space=pltpu.VMEM)
     full = (tokens, channels)
-    gs, gc, gp, small = pl.pallas_call(
+    fin, small = pl.pallas_call(
         functools.partial(kernel, n, g, count),
         out_shape=(
-            jax.ShapeDtypeStruct((w_second.shape[0] // n, channels), F32),
-            jax.ShapeDtypeStruct((w_context.shape[0] // n, channels), F32),
-            jax.ShapeDtypeStruct((horizons, channels // n, channels), F32),
+            jax.ShapeDtypeStruct((pieces, g, prow, cols), BF16),
             jax.ShapeDtypeStruct((16, channels), F32),
         ),
         in_specs=[spec] * 7,
-        out_specs=[spec] * 4,
+        out_specs=[spec] * 2,
         scratch_shapes=[
+            vm((quarters, LANES, channels), BF16),
             vm((quarters,) + full, BF16),
             vm(full, F32),
             vm(full, F32),
@@ -451,7 +464,8 @@
             vm(full, F32),
             vm((2,) + full, BF16),
             vm((2,) + full, BF16),
-            vm((LANES, channels), F32),
+            vm((quarters, LANES, channels), F32),
+            vm((quarters, LANES, channels), F32),
             vm((n, picks, channels), BF16),
             vm((n, picks, channels), BF16),
             vm((n, picks, channels), BF16),
@@ -461,7 +475,6 @@
             vm((pieces, 2, chips, prow, channels), BF16),
             vm((pieces, chips, prow, channels), BF16),
             vm((pieces, chips, prow, channels), BF16),
-            vm((pieces, g, prow, cols), BF16),
             vm((pieces, g, prow, cols), BF16),
             vm((pieces, g, prow, cols), BF16),
         ]
@@ -474,15 +487,28 @@
             collective_id=0, has_side_effects=True, vmem_limit_bytes=56 * 1024 * 1024
         ),
     )(
-        offs,
-        xq,
-        w1,
+        offsets,
+        x,
+        w_first,
         w_second.reshape(2 * quarters, channels, channels),
         gain.reshape(1, channels),
         w_context.reshape(2, channels, channels),
         w_predict,
     )
-    return (small[11, 0] / count, small[:10], gs, small[10], gc, gp)
+    loss, gf, gs, gg, gc, gp = pl.pallas_call(
+        functools.partial(finish, count),
+        out_shape=(
+            jax.ShapeDtypeStruct((1, 1), F32),
+            jax.ShapeDtypeStruct(w_first.shape, F32),
+            jax.ShapeDtypeStruct((w_second.shape[0] // n, channels), F32),
+            jax.ShapeDtypeStruct((1, channels), F32),
+            jax.ShapeDtypeStruct((w_context.shape[0] // n, channels), F32),
+            jax.ShapeDtypeStruct((horizons, channels // n, channels), F32),
+        ),
+        in_specs=[spec] * 2,
+        out_specs=[spec] * 6,
+    )(fin, small)
+    return (loss.reshape(()), gf, gs, gg.reshape(channels), gc, gp)
 
 
 def solution(mesh):

time: 121 us -> 104 us (0.86)
  local copies, waits for them, and re-layouts: 16.4 us -> 6.24 us
  between operations: 8.32 us -> 0.67 us
  Pallas kernels: 94.8 us -> 97 us
    unnamed x11 -> x3, local copies, waits for them, and re-layouts: 7.82 us -> 0.25 us
    slice x4 -> x1, local copies, waits for them, and re-layouts: 3.86 us -> 1.35 us  [frame_inputs(): starts[w]]
    pallas_call x0 -> x1, Pallas kernels: none -> 2.45 us  [on_device(): pl.pallas_call(functools.partial(finish, count), out_shape=(jax.ShapeDtyp...]
    dynamic_slice x1, local copies, waits for them, and re-layouts: 0.89 us -> 2.91 us  [frame_inputs(): lax.dynamic_slice(audio, (jnp.int32(0), starts[w]), (1, span), allow_nega...]
    reshape x1 -> x0, local copies, waits for them, and re-layouts: 1.4 us -> none  [on_device(): offs = offsets.reshape(picks, 1)]
where the time goes in v2:
time: 104 us
  Pallas kernels  97 us (93%)
  local copies, waits for them, and re-layouts  6.24 us (6%)
    pallas_call x1, Pallas kernels, on_device(): pl.pallas_call(functools.partial(kernel, n, g, count), out_shape=(jax.Sha...  94.6 us
    dynamic_slice x1, local copies, waits for them, and re-layouts, frame_inputs(): lax.dynamic_slice(audio, (jnp.int32(0), starts[w]), (1, span), allow_nega...  2.91 us
    pallas_call x1, Pallas kernels, on_device(): pl.pallas_call(functools.partial(finish, count), out_shape=(jax.ShapeDtyp...  2.45 us

profile of v2, /device:TPU:0, one launch (start us, length us, event | category | flops | bytes accessed | tf_op | source)
XLA Modules:
  0.0 104.0 jit_solution(9753240718302286435)
XLA Ops:
  0.6 1.4 %fusion.15 = (s32[1]{0:T(128)}, s32[1]{0:T(128)}, s32[1]{0:T(128)}) fusion(s32[3]{0:T(128)} %param.9), kind=kLoop, calls=%fused_computation.23 | loop fusion | bytes 24 | tf_op jit(solution)/shard_map/slice | solution.py:413
  2.0 2.9 %dynamic-slice_reduce_fusion.2 = (bf16[2560]{0:T(1024)(128)(2,1)S(1)}, bf16[2560]{0:T(1024)(128)(2,1)S(1)}, bf16[2560]{0:T(1024)(128)(2,1)S(1)}) fusion(bf16[1,15360]{1,0:T(2,128)(2,1)} %param.8, s32[]{:T(128)} %bitcast, s32[]{:T(128)} %bitcast.2, s32[]{:T(128)} %bitcast.1), kind=kLoop, calls=%fused_computation.22 | loop fusion | bytes 30732 | tf_op jit(solution)/shard_map/dynamic_slice | solution.py:412
  4.9 0.1 reshape.36
  5.0 0.1 copy.15
  5.1 0.1 slice.24
  5.2 0.1 copy.21
  5.3 0.1 reshape.38
  5.4 0.1 copy.19
  5.5 0.1 slice.26
  5.6 0.1 copy.23
  5.7 0.1 reshape.37
  5.8 0.1 copy.17
  5.9 0.1 slice.25
  6.0 0.1 copy.22
  6.1 0.1 fusion.12
  6.2 0.1 copy.20
  6.3 0.7 pad.7.x_ref
  7.0 94.6 %shard_map.127 = (bf16[6,4,128,128]{3,2,1,0:T(8,128)(2,1)}, f32[16,512]{1,0:T(8,128)}) custom-call(s32[1,2,32]{2,1,0:T(2,128)} %offs_ref.1, bf16[384,128]{1,0:T(8,128)(2,1)} %pad.7.x_ref, bf16[10,512]{1,0:T(8,128)(2,1)} %first_ref.1, bf16[8,512,512]{2,1,0:T(8,128)(2,1)} %bitcast.8, f32[1,512]{1,0:T(1,128)} %bitcast.10, bf16[2,512,512]{2,1,0:T(8,128)(2,1)} %bitcast.9, ...), custom_call_target="tpu_custom_call" | custom-call | tf_op jit(solution)/shard_map/pallas_call | solution.py:441
  101.6 2.5 %shard_map.128 = (f32[1,1]{1,0:T(1,128)}, f32[10,512]{1,0:T(8,128)}, f32[512,512]{1,0:T(8,128)}, f32[1,512]{1,0:T(1,128)}, f32[128,512]{1,0:T(8,128)}, /*index=5*/f32[2,64,512]{2,1,0:T(8,128)}) custom-call(bf16[6,4,128,128]{3,2,1,0:T(8,128)(2,1)} %get-tuple-element.14.fin_ref, f32[16,512]{1,0:T(8,128)} %get-tuple-element.15.small_ref), custom_call_target="tpu_custom_call" | custom-call | tf_op jit(solution)/shard_map/pallas_call | solution.py:498

commit v3 on v2

--- a/solution.py
+++ b/solution.py
@@ -259,6 +259,7 @@
         for parity in range(2):
             stage[1, parity, half * (chips // 2) : (half + 1) * (chips // 2)] = share[:, parity]
     core_copy(1).start()
+    core_done(0)
     acc_a[...] = dot_nt(cgv[1], wc_ref[1]) + dot_nt(cgv[0], wc_ref[0])
 
     each(n, lambda j: own_copy(j, dp_peer(j)).wait_recv())
@@ -271,7 +272,6 @@
     for k in range(horizons):
         mine = slice(k * per, (k + 1) * per)
         acc_b[...] += dot(chosen[k], high[mine]) + dot(chosen[k], low[mine])
-    core_done(0)
     core_done(1)
     small_in[me] = jnp.zeros_like(small_in[me])
 
@@ -337,6 +337,7 @@
         return carry
 
     lax.fori_loop(0, quarters, first, 0)
+    chip_done(2)
     row = lax.broadcasted_iota(jnp.int32, (16, channels), 0)
     gain_row = small_in[me, 0:1]
     first_sum = gfirst[0, 0:16, :]
@@ -355,20 +356,18 @@
         return to_z(small_z.at[slot], small_z.at[slot], sz_s.at[j], sz_r.at[slot], z_peer(j))
 
     each(n, lambda j: small_copy(j, me).start())
-    chip_done(2)
     z_done(0)
     z_done(1)
+    for p in range(3, pieces):
+        chip_done(p)
+        z_done(p - 1)
     each(n, lambda j: small_copy(j, dp_peer(j)).wait_recv())
     small_z[zme] = lax.fori_loop(1, n, lambda j, total: total + small_in[j], small_in[0])
     each(g, lambda j: small_z_copy(j, zme).start())
-    for p in range(3, pieces):
-        chip_done(p)
-        z_done(p - 1)
-        fin_done(p - 3)
     z_done(pieces - 1)
     each(g, lambda j: small_z_copy(j, z_peer(j)).wait_recv())
     small_ref[...] = lax.fori_loop(1, g, lambda j, total: total + small_z[j], small_z[0])
-    for p in range(pieces - 3, pieces):
+    for p in range(pieces):
         fin_done(p)
 
     def leave_dp(j):

time: 104 us -> 91.3 us (0.88)
  Pallas kernels: 97 us -> 84 us
    pallas_call x1, Pallas kernels: 94.6 us -> 81.6 us  [on_device(): pl.pallas_call(functools.partial(kernel, n, g, count), out_shape=(jax.Sha...]
where the time goes in v3:
time: 91.3 us; the launch traced here: 91 us
  Pallas kernels  84 us (92%)
  local copies, waits for them, and re-layouts  6.2 us (7%)
    pallas_call x1, Pallas kernels, on_device(): pl.pallas_call(functools.partial(kernel, n, g, count), out_shape=(jax.Sha...  81.6 us
    dynamic_slice x1, local copies, waits for them, and re-layouts, frame_inputs(): lax.dynamic_slice(audio, (jnp.int32(0), starts[w]), (1, span), allow_nega...  2.87 us
    pallas_call x1, Pallas kernels, on_device(): pl.pallas_call(functools.partial(finish, count), out_shape=(jax.ShapeDtyp...  2.45 us

profile of v3, /device:TPU:0, one launch (start us, length us, event | category | flops | bytes accessed | tf_op | source)
XLA Modules:
  0.0 91.0 jit_solution(6362886862809307658)
XLA Ops:
  0.6 1.4 %fusion.15 = (s32[1]{0:T(128)}, s32[1]{0:T(128)}, s32[1]{0:T(128)}) fusion(s32[3]{0:T(128)} %param.9), kind=kLoop, calls=%fused_computation.23 | loop fusion | bytes 24 | tf_op jit(solution)/shard_map/slice | solution.py:412
  2.0 2.9 %dynamic-slice_reduce_fusion.2 = (bf16[2560]{0:T(1024)(128)(2,1)S(1)}, bf16[2560]{0:T(1024)(128)(2,1)S(1)}, bf16[2560]{0:T(1024)(128)(2,1)S(1)}) fusion(bf16[1,15360]{1,0:T(2,128)(2,1)} %param.8, s32[]{:T(128)} %bitcast, s32[]{:T(128)} %bitcast.2, s32[]{:T(128)} %bitcast.1), kind=kLoop, calls=%fused_computation.22 | loop fusion | bytes 30732 | tf_op jit(solution)/shard_map/dynamic_slice | solution.py:411
  4.9 0.1 reshape.36
  5.0 0.1 copy.15
  5.1 0.1 slice.24
  5.2 0.1 copy.21
  5.2 0.1 reshape.38
  5.4 0.1 copy.19
  5.5 0.1 slice.26
  5.6 0.1 copy.23
  5.6 0.1 reshape.37
  5.8 0.1 copy.17
  5.9 0.1 slice.25
  6.0 0.1 copy.22
  6.1 0.1 fusion.12
  6.2 0.1 copy.20
  6.3 0.7 pad.7.x_ref
  7.0 81.6 %shard_map.127 = (bf16[6,4,128,128]{3,2,1,0:T(8,128)(2,1)}, f32[16,512]{1,0:T(8,128)}) custom-call(s32[1,2,32]{2,1,0:T(2,128)} %offs_ref.1, bf16[384,128]{1,0:T(8,128)(2,1)} %pad.7.x_ref, bf16[10,512]{1,0:T(8,128)(2,1)} %first_ref.1, bf16[8,512,512]{2,1,0:T(8,128)(2,1)} %bitcast.8, f32[1,512]{1,0:T(1,128)} %bitcast.10, bf16[2,512,512]{2,1,0:T(8,128)(2,1)} %bitcast.9, ...), custom_call_target="tpu_custom_call" | custom-call | tf_op jit(solution)/shard_map/pallas_call | solution.py:440
  88.5 2.5 %shard_map.128 = (f32[1,1]{1,0:T(1,128)}, f32[10,512]{1,0:T(8,128)}, f32[512,512]{1,0:T(8,128)}, f32[1,512]{1,0:T(1,128)}, f32[128,512]{1,0:T(8,128)}, /*index=5*/f32[2,64,512]{2,1,0:T(8,128)}) custom-call(bf16[6,4,128,128]{3,2,1,0:T(8,128)(2,1)} %get-tuple-element.14.fin_ref, f32[16,512]{1,0:T(8,128)} %get-tuple-element.15.small_ref), custom_call_target="tpu_custom_call" | custom-call | tf_op jit(solution)/shard_map/pallas_call | solution.py:497

commit v4 on v3

--- a/solution.py
+++ b/solution.py
@@ -236,9 +236,10 @@
         each(g, lambda j: fin_copy(p, j, z_peer(j)).wait_recv())
 
     shares = []
+    turned_context = context[...].T
     for k in range(horizons):
         qg[k] = (posq[k] + dot(negw[k], panel_rows(k))).astype(BF16)
-        shares.append(dot_tn(context[...], qg[k]).reshape(n, channels // n, channels))
+        shares.append(dot(turned_context, qg[k]).reshape(n, channels // n, channels))
     joined = jnp.concatenate(shares, axis=1).astype(BF16).reshape(chips, 2, prow, channels)
     for parity in range(2):
         stage[0, parity] = joined[:, parity]
@@ -254,8 +255,9 @@
         cgv[0, rows, :] = earlier(rounded.astype(F32), 1).astype(BF16)
 
     windows(make_context_grad)
+    turned_latent = latent[...].T
     for half in range(2):
-        share = dot_tn(latent[...], cgv[half]).astype(BF16).reshape(chips // 2, 2, prow, channels)
+        share = dot(turned_latent, cgv[half]).astype(BF16).reshape(chips // 2, 2, prow, channels)
         for parity in range(2):
             stage[1, parity, half * (chips // 2) : (half + 1) * (chips // 2)] = share[:, parity]
     core_copy(1).start()
@@ -301,14 +303,19 @@
     if prow == LANES:
         for i in range(seconds):
 
-            def fill(b, carry, i=i):
-                stage[2 + i, lax.rem(b, 2), b // 2] = second(b, i)
-                return carry
-
-            lax.fori_loop(0, 2 * quarters, fill, 0)
+            def fill(parity, i=i):
+                for h in range(quarters // 2):
+                    turned = hid[2 * h + parity, :, i * LANES : (i + 1) * LANES].T
+                    for v in range(2):
+                        stage[2 + i, parity, h + v * (quarters // 2)] = dot(turned, pv[v]).astype(BF16)
+
+            fill(1 - my_core)
             core_copy(2 + i).start()
+            fill(my_core)
             if i > 0:
                 core_done(1 + i)
+            if i > 1:
+                chip_done(i - 2)
     else:
         each_chips = LANES // (seconds * prow) // 2
 
@@ -327,8 +334,9 @@
             if i > 0:
                 core_done(1 + i)
     core_done(pieces - 1)
-    chip_done(0)
-    chip_done(1)
+    if prow != LANES:
+        chip_done(0)
+        chip_done(1)
 
     def first(q, carry):
         back = dot_nt(pv[1], w2_ref[q + quarters]) + dot_nt(pv[0], w2_ref[q])
@@ -336,8 +344,13 @@
         gfirst[q] = dot_tn(x_ref[...], jnp.where(pre > 0, back, 0.0).astype(BF16))
         return carry
 
-    lax.fori_loop(0, quarters, first, 0)
+    lax.fori_loop(0, quarters // 2, first, 0)
+    z_done(0)
+    z_done(1)
     chip_done(2)
+    lax.fori_loop(quarters // 2, quarters, first, 0)
+    chip_done(3)
+    z_done(2)
     row = lax.broadcasted_iota(jnp.int32, (16, channels), 0)
     gain_row = small_in[me, 0:1]
     first_sum = gfirst[0, 0:16, :]
@@ -356,9 +369,7 @@
         return to_z(small_z.at[slot], small_z.at[slot], sz_s.at[j], sz_r.at[slot], z_peer(j))
 
     each(n, lambda j: small_copy(j, me).start())
-    z_done(0)
-    z_done(1)
-    for p in range(3, pieces):
+    for p in range(4, pieces):
         chip_done(p)
         z_done(p - 1)
     each(n, lambda j: small_copy(j, dp_peer(j)).wait_recv())

time: 91.3 us -> 88.1 us (0.965)
  Pallas kernels: 84 us -> 80.9 us
    pallas_call x1, Pallas kernels: 81.6 us -> 78.4 us  [on_device(): pl.pallas_call(functools.partial(kernel, n, g, count), out_shape=(jax.Sha...]
where the time goes in v4:
time: 88.1 us; the launch traced here: 87.8 us
  Pallas kernels  80.9 us (92%)
  local copies, waits for them, and re-layouts  6.16 us (7%)
    pallas_call x1, Pallas kernels, on_device(): pl.pallas_call(functools.partial(kernel, n, g, count), out_shape=(jax.Sha...  78.4 us
    dynamic_slice x1, local copies, waits for them, and re-layouts, frame_inputs(): lax.dynamic_slice(audio, (jnp.int32(0), starts[w]), (1, span), allow_nega...  2.83 us
    pallas_call x1, Pallas kernels, on_device(): pl.pallas_call(functools.partial(finish, count), out_shape=(jax.ShapeDtyp...  2.45 us

profile of v4, /device:TPU:0, one launch (start us, length us, event | category | flops | bytes accessed | tf_op | source)
XLA Modules:
  0.0 87.8 jit_solution(17451255287533526493)
XLA Ops:
  0.6 1.4 %fusion.15 = (s32[1]{0:T(128)}, s32[1]{0:T(128)}, s32[1]{0:T(128)}) fusion(s32[3]{0:T(128)} %param.9), kind=kLoop, calls=%fused_computation.23 | loop fusion | bytes 24 | tf_op jit(solution)/shard_map/slice | solution.py:423
  2.0 2.8 %dynamic-slice_reduce_fusion.2 = (bf16[2560]{0:T(1024)(128)(2,1)S(1)}, bf16[2560]{0:T(1024)(128)(2,1)S(1)}, bf16[2560]{0:T(1024)(128)(2,1)S(1)}) fusion(bf16[1,15360]{1,0:T(2,128)(2,1)} %param.8, s32[]{:T(128)} %bitcast, s32[]{:T(128)} %bitcast.2, s32[]{:T(128)} %bitcast.1), kind=kLoop, calls=%fused_computation.22 | loop fusion | bytes 30732 | tf_op jit(solution)/shard_map/dynamic_slice | solution.py:422
  4.8 0.1 reshape.36
  4.9 0.1 copy.15
  5.0 0.1 slice.24
  5.1 0.1 copy.21
  5.2 0.1 reshape.38
  5.3 0.1 copy.19
  5.4 0.1 slice.26
  5.5 0.1 copy.23
  5.6 0.1 reshape.37
  5.8 0.1 copy.17
  5.8 0.1 slice.25
  5.9 0.1 copy.22
  6.0 0.1 fusion.12
  6.1 0.1 copy.20
  6.3 0.7 pad.7.x_ref
  6.9 78.4 %shard_map.127 = (bf16[6,4,128,128]{3,2,1,0:T(8,128)(2,1)}, f32[16,512]{1,0:T(8,128)}) custom-call(s32[1,2,32]{2,1,0:T(2,128)} %offs_ref.1, bf16[384,128]{1,0:T(8,128)(2,1)} %pad.7.x_ref, bf16[10,512]{1,0:T(8,128)(2,1)} %first_ref.1, bf16[8,512,512]{2,1,0:T(8,128)(2,1)} %bitcast.8, f32[1,512]{1,0:T(1,128)} %bitcast.10, bf16[2,512,512]{2,1,0:T(8,128)(2,1)} %bitcast.9, ...), custom_call_target="tpu_custom_call" | custom-call | tf_op jit(solution)/shard_map/pallas_call | solution.py:451
  85.4 2.5 %shard_map.128 = (f32[1,1]{1,0:T(1,128)}, f32[10,512]{1,0:T(8,128)}, f32[512,512]{1,0:T(8,128)}, f32[1,512]{1,0:T(1,128)}, f32[128,512]{1,0:T(8,128)}, /*index=5*/f32[2,64,512]{2,1,0:T(8,128)}) custom-call(bf16[6,4,128,128]{3,2,1,0:T(8,128)(2,1)} %get-tuple-element.14.fin_ref, f32[16,512]{1,0:T(8,128)} %get-tuple-element.15.small_ref), custom_call_target="tpu_custom_call" | custom-call | tf_op jit(solution)/shard_map/pallas_call | solution.py:508
